TPU v7x, 512 devices: a whole 4x8x8 slice. The times are simulated.
512 devices in a mesh: row: 8 (over x, core), col: 16 (over y_lo, z), layer: 4 (over y_hi).
Axes of the slice: x: 4, y: 8 (y_hi: 4, y_lo: 2; y = y_hi * 2 + y_lo), z: 8, core: 2. Of those that a mesh axis runs over, the one named last changes fastest.
Arguments:
- hamiltonian: bfloat16 [8192, 8192], P('row', ('col', 'layer')), as said below
- inv_root: bfloat16 [8192, 8192], P('row', 'col'), as said below
- h_pattern: int32 [32, 32], replicated, may hold values from 0 to 1, as said below
- z_pattern: int32 [32, 32], replicated, may hold values from 0 to 1, as said below
Outputs:
- transformed: bfloat16 [8192, 8192], P('row', ('col', 'layer'))
Inputs may be any that keep to these rules, and one draw needn't show every extreme that they name: hamiltonian is symmetric. inv_root is symmetric. h_pattern is symmetric and every diagonal block is present. z_pattern is symmetric and every diagonal block is present.
All inputs are finite; a program needn't handle non-finite values.
Results may differ from a plain program's by a relative error of at most 0.005.
Values may be sent and summed in bfloat16 or wider, within the bound.
A program may use at most 64 MiB of HBM per device.

v0:
```python
import jax
import jax.numpy as jnp
from jax import lax
from jax.sharding import PartitionSpec as P

BS = 256


def mask_tile(tile, pattern, row_start, col_start):
    blocks = pattern.shape[0]
    block_ids = jnp.arange(blocks, dtype=jnp.int32)
    row_ids = (row_start + jnp.arange(tile.shape[0], dtype=jnp.int32)) // BS
    col_ids = (col_start + jnp.arange(tile.shape[1], dtype=jnp.int32)) // BS
    row_pick = (row_ids[:, None] == block_ids[None, :]).astype(jnp.float32)
    col_pick = (block_ids[:, None] == col_ids[None, :]).astype(jnp.float32)
    inner = jnp.dot(pattern.astype(jnp.float32), col_pick, precision=lax.Precision.HIGHEST)
    keep = jnp.dot(row_pick, inner, precision=lax.Precision.HIGHEST)
    return jnp.where(keep > 0.5, tile, jnp.zeros_like(tile))


def accumulate(left, right):
    return jnp.dot(left, right, preferred_element_type=jnp.float32)


def local(hamiltonian, inv_root, h_pattern, z_pattern):
    rows_here = inv_root.shape[0]
    cols_here = inv_root.shape[1]
    quarter = hamiltonian.shape[1]
    layers = lax.axis_size("layer")
    per_row = lax.axis_size("col") // lax.axis_size("row")
    row_index = lax.axis_index("row")
    col_index = lax.axis_index("col")
    layer_index = lax.axis_index("layer")
    h_local = mask_tile(
        hamiltonian, h_pattern, row_index * rows_here, col_index * cols_here + layer_index * quarter
    )
    z_local = mask_tile(inv_root, z_pattern, row_index * rows_here, col_index * cols_here)
    h_whole = lax.all_gather(h_local, "col", axis=1, tiled=True)
    z_layered = z_local.reshape(per_row, layers, quarter, cols_here)
    z_part = lax.dynamic_index_in_dim(z_layered, layer_index, 1, keepdims=False).reshape(
        per_row * quarter, cols_here
    )
    columns = h_whole
    partial_y = accumulate(columns, lax.all_gather(z_part, "row", axis=0, tiled=True))
    z_quarter = lax.dynamic_slice_in_dim(z_local, layer_index * quarter, quarter, 1)
    z_rows = lax.all_gather(z_quarter, "col", axis=1, tiled=True)
    summed = lax.psum(partial_y, "layer")
    layered = summed.reshape(per_row, layers, quarter, cols_here)
    own_rows = lax.dynamic_index_in_dim(layered, layer_index, 1, keepdims=False).reshape(
        per_row * quarter, cols_here
    )
    y_own = own_rows.astype(jnp.bfloat16)
    columns = z_rows
    partial_c = accumulate(columns, lax.all_gather(y_own, "row", axis=0, tiled=True))
    result = lax.psum_scatter(partial_c, "layer", scatter_dimension=1, tiled=True)
    return result.astype(jnp.bfloat16)


def solution(mesh):
    return jax.shard_map(
        local,
        mesh=mesh,
        in_specs=(P("row", ("col", "layer")), P("row", "col"), P(), P()),
        out_specs=P("row", ("col", "layer")),
        check_vma=False,
    )
```

profile of v0, /device:TPU:1, one launch (start us, length us, event | category | flops | bytes accessed | tf_op | source)
XLA Modules:
  0.0 365.4 jit_solution(18108361089963021768)
XLA Ops:
  6.6 1.1 fusion.4
  7.7 2.3 compare_select_fusion
  10.0 0.7 constant_dynamic-slice_fusion
  10.7 0.0 all-gather.9.cloned.1.call-update
  10.7 0.0 all-gather.7.cloned.1.call-start
  10.8 0.2 fusion.7
  11.1 1.2 fusion
  12.3 0.0 all-gather.7.cloned.1.call-update
  12.3 0.0 all-gather.5.cloned.1.call-start
  12.3 0.7 constant_dynamic-slice_fusion.1
  13.1 0.0 all-gather.5.cloned.1.call-update
  13.1 0.0 all-gather.11.cloned.1.call-start
  13.1 34.1 %all-gather.9.cloned.1.call-done = bf16[2048,512]{1,0:T(8,128)(2,1)} async-done(((bf16[256,512]{1,0:T(8,128)(2,1)}), bf16[2048,512]{1,0:T(8,128)(2,1)}) %all-gather.9.cloned.1.call-update) | async-done | bytes 2097168 | tf_op jit(solution)/shard_map/all_gather | solution.py:44
  47.3 84.6 %all-gather.7.cloned.1.call-done = bf16[1024,2048]{1,0:T(8,128)(2,1)} async-done(((bf16[1024,128]{1,0:T(8,128)(2,1)}), bf16[1024,2048]{1,0:T(8,128)(2,1)}) %all-gather.7.cloned.1.call-update) | async-done | bytes 4194320 | tf_op jit(solution)/shard_map/all_gather | solution.py:38
  131.9 5.2 %fusion.19 = f32[1024,512]{1,0:T(8,128)S(1)} fusion(bf16[1024,2048]{1,0:T(8,128)(2,1)} %all-gather.7.cloned.1.call-done, bf16[2048,512]{1,0:T(8,128)(2,1)} %all-gather.9.cloned.1.call-done), kind=kOutput, calls=%fused_computation.41 | convolution fusion | flops 2147483648 | bytes 8388608 | tf_op jit(solution)/shard_map/dot_general | solution.py:22
  137.1 85.9 %all-reduce.1 = bf16[2,4,128,512]{3,2,1,0:T(8,128)(2,1)S(1)} all-reduce(f32[2,4,128,512]{3,2,1,0:T(8,128)S(1)} %bitcast.10), channel_id=1, replica_groups=mesh['row'=8,'col'=16,'layer'=4] {'layer'}, use_global_device_ids=true, to_apply=%region_0.1 | all-reduce | flops 524288 | bytes 3145728 | tf_op jit(solution)/shard_map/psum | solution.py:47
  223.0 0.7 dynamic-slice_convert_fusion
  223.7 0.0 reduce-scatter.2.cloned.1.call-start
  223.8 38.3 %all-gather.5.cloned.1.call-done = bf16[1024,2048]{1,0:T(8,128)(2,1)} async-done(((bf16[1024,128]{1,0:T(8,128)(2,1)}), bf16[1024,2048]{1,0:T(8,128)(2,1)}) %all-gather.5.cloned.1.call-update) | async-done | bytes 4194320 | tf_op jit(solution)/shard_map/all_gather | solution.py:46
  262.1 36.0 %all-gather.11.cloned.1.call-done = bf16[2048,512]{1,0:T(8,128)(2,1)} async-done(((bf16[256,512]{1,0:T(8,128)(2,1)}), bf16[2048,512]{1,0:T(8,128)(2,1)}) %all-gather.11.cloned.1.call-update) | async-done | bytes 2097168 | tf_op jit(solution)/shard_map/all_gather | solution.py:54
  298.1 6.5 %fusion.20 = f32[1024,512]{1,0:T(8,128)} fusion(bf16[1024,2048]{1,0:T(8,128)(2,1)} %all-gather.5.cloned.1.call-done, bf16[2048,512]{1,0:T(8,128)(2,1)} %all-gather.11.cloned.1.call-done), kind=kOutput, calls=%fused_computation.42 | convolution fusion | flops 2147483648 | bytes 8388608 | tf_op jit(solution)/shard_map/dot_general | solution.py:22
  304.6 0.0 reduce-scatter.2.cloned.1.call-update
  304.6 52.5 %reduce-scatter.2.cloned.1.call-done = f32[1024,128]{1,0:T(8,128)} async-done(((f32[1024,512]{1,0:T(8,128)}), f32[1024,128]{1,0:T(8,128)}) %reduce-scatter.2.cloned.1.call-update) | async-done | bytes 524304 | tf_op jit(solution)/shard_map/reduce_scatter | solution.py:55
  357.1 1.8 convert_element_type.23
  (9 shorter events, 0.1 us)
Async XLA Ops:
  6.5 4.3 %copy-start = (s32[32,32]{1,0:T(8,128)S(1)}, s32[32,32]{1,0:T(8,128)}, u32[]{:S(2)}) copy-start(s32[32,32]{1,0:T(8,128)} %param.6) | copy-start | bytes 12292
  6.5 4.5 %copy-start.1 = (bf16[1024,128]{1,0:T(8,128)(2,1)S(1)}, bf16[1024,128]{1,0:T(8,128)(2,1)}, u32[]{:S(2)}) copy-start(bf16[1024,128]{1,0:T(8,128)(2,1)} %param.4) | copy-start | bytes 786436
  6.5 40.7 %all-gather.9.cloned.1.call-start = ((), (), s32[]{:S(2)}) async-start(), calls=%async_computation.3 | async-start | bytes 2359296 | tf_op jit(solution)/shard_map/all_gather | solution.py:44
  10.7 121.2 %all-gather.7.cloned.1.call-start = ((), (), s32[]{:S(2)}) async-start(), calls=%async_computation.2 | async-start | bytes 4456448 | tf_op jit(solution)/shard_map/all_gather | solution.py:38
  12.3 249.8 %all-gather.5.cloned.1.call-start = ((), (), s32[]{:S(2)}) async-start(), calls=%async_computation.1 | async-start | bytes 4456448 | tf_op jit(solution)/shard_map/all_gather | solution.py:46
  13.1 285.0 %all-gather.11.cloned.1.call-start = ((), (), s32[]{:S(2)}) async-start(), calls=%async_computation.4 | async-start | bytes 2359296 | tf_op jit(solution)/shard_map/all_gather | solution.py:54
  223.7 133.4 %reduce-scatter.2.cloned.1.call-start = ((), (), s32[]{:S(2)}) async-start(), calls=%async_computation.5 | async-start | bytes 2621440 | tf_op jit(solution)/shard_map/reduce_scatter | solution.py:55
Sparse Core Ops, SparseCore 0:
  10.9 36.3 all-gather.8
  49.3 82.5 all-gather.6
  133.9 128.0 all-gather.4
  264.1 33.9 all-gather.10
  304.8 52.3 reduce-scatter.1
where the time goes:
time: 366 us; the launch traced here: 365 us
  waiting for transfers between devices  246 us (67%)
  blocking collectives  85.9 us (23%)
  matrix products  16.5 us (5%)
  between operations  13.2 us (4%)
    psum x1, blocking collectives, local(): summed = lax.psum(partial_y, 'layer')  85.9 us
    all_gather x1, waiting for transfers between devices, local(): h_whole = lax.all_gather(h_local, 'col', axis=1, tiled=True)  84.6 us
    reduce_scatter x1, waiting for transfers between devices, local(): lax.psum_scatter(partial_c, 'layer', scatter_dimension=1, tiled=True)  52.5 us
    all_gather x1, waiting for transfers between devices, local(): z_rows = lax.all_gather(z_quarter, 'col', axis=1, tiled=True)  38.3 us
    all_gather x1, waiting for transfers between devices, local(): lax.all_gather(y_own, 'row', axis=0, tiled=True)  36 us
    all_gather x1, waiting for transfers between devices, local(): lax.all_gather(z_part, 'row', axis=0, tiled=True)  34.1 us
    dot_general x2, matrix products, accumulate(): return jnp.dot(left, right, preferred_element_type=jnp.float32)  11.7 us
  transfers between devices with their start and end apart: 5, of which 5 were waited for; matrix products, arithmetic and copies ran while one was open for 2% of the time, Pallas kernels for 0%

commit v1 on v0

v1 whole, which is shorter than its diff:
```python
import functools
import jax
import jax.numpy as jnp
from jax import lax
from jax.experimental import pallas as pl
from jax.experimental.pallas import tpu as pltpu
from jax.sharding import PartitionSpec as P

BS = 256
BF = jnp.bfloat16
F32 = jnp.float32
MESH = pl.DeviceIdType.MESH

SRC = ((0, 1, 3, 5), (0, 2, 4, 6))
DST = ((1, 3, 5, 7), (2, 4, 6, 7))

UNITS = {"u0": (0, 128), "u1": (128, 256), "u2": (384, 256), "v": (0, 640), "u3": (640, 256), "u4": (896, 128)}


def body(hp, zp, h_ref, z_ref, o_ref, ht, z1, z2, y, pbuf, xbuf, rss, rsr, cpart, csend, crecv,
         hs, hr, z1s, z1r, z2s, z2r, ks, kr, rs_s, rs_r, ag_s, ag_r, fs, fr, cs, cr):
    row = lax.axis_index("row")
    col = lax.axis_index("col")
    layer = lax.axis_index("layer")
    x, c = row // 2, lax.rem(row, 2)
    y_lo, z = col // 8, lax.rem(col, 8)
    y_pos = layer * 2 + y_lo

    def at_z(d):
        return {"col": y_lo * 8 + lax.rem(z + d + 8, 8)}

    def at_y(d):
        t = lax.rem(y_pos + d + 8, 8)
        return {"col": lax.rem(t, 2) * 8 + z, "layer": t // 2}

    def at_x(d):
        return {"row": lax.rem(x + d + 4, 4) * 2 + c}

    zdev = (at_z(1), at_z(-1))
    ydev = (at_y(1), at_y(-1))
    xdev = (at_x(1), at_x(2), at_x(3))
    sib = {"row": x * 2 + 1 - c}

    barrier = pltpu.get_barrier_semaphore()
    for d in (*zdev, *ydev, *xdev, sib):
        pl.semaphore_signal(barrier, inc=1, device_id=d, device_id_type=MESH)

    pending = []

    def rcopy(src, dst, s, r, dev):
        return pltpu.make_async_remote_copy(
            src_ref=src, dst_ref=dst, send_sem=s, recv_sem=r, device_id=dev, device_id_type=MESH
        )

    def go(cp):
        cp.start()
        pending.append(cp)

    for i in range(4):
        p = hp[row * 4 + i, col * 2 + layer // 2]
        keep = jnp.where(p > 0, 1.0, 0.0).astype(F32)
        blk = h_ref[i * BS:(i + 1) * BS, :].astype(F32) * keep
        ht[0:128, i * BS:(i + 1) * BS] = blk.T.astype(BF)

    pl.semaphore_wait(barrier, 8)

    def h_copy(d, s, j):
        return rcopy(
            ht.at[pl.ds(SRC[d][s] * 128 + j * 32, 32)], ht.at[pl.ds(DST[d][s] * 128 + j * 32, 32)],
            hs.at[d, s, j], hr.at[d, s, j], zdev[d],
        )

    for j in range(4):
        for d in range(2):
            go(h_copy(d, 0, j))

    for i in range(4):
        for k in range(2):
            p = zp[row * 4 + i, col * 2 + k]
            keep = jnp.where(p > 0, 1.0, 0.0).astype(F32)
            blk = z_ref[i * BS:(i + 1) * BS, k * BS:(k + 1) * BS].astype(F32) * keep
            z1[y_lo, i * BS:(i + 1) * BS, k * BS:(k + 1) * BS] = blk.astype(BF)

    def z1_copy(d, who):
        part = z1.at[who, pl.ds(d * 512, 512)]
        return rcopy(part, part, z1s.at[d], z1r.at[d], ydev[d])

    for d in range(2):
        go(z1_copy(d, y_lo))
    z2[0] = z1[y_lo, :, pl.ds(pl.multiple_of(layer * 128, 128), 128)]

    def z2_copy(d, s, j):
        start, size = j * 256, 256
        if s == 3:
            start, size = start + d * 128, 128
        return rcopy(
            z2.at[SRC[d][s], pl.ds(start, size)], z2.at[DST[d][s], pl.ds(start, size)],
            z2s.at[d, s, j], z2r.at[d, s, j], zdev[d],
        )

    def h_arrive(s, j):
        for d in range(2):
            h_copy(d, s, j).wait_recv()
            if s < 2 or (s == 2 and j // 2 == d):
                go(h_copy(d, s + 1, j))

    def h_last(j):
        for d in range(2):
            h_copy(d, 3, j + 2 * d).wait_recv()

    def z2_start(js):
        for j in js:
            for d in range(2):
                go(z2_copy(d, 0, j))

    def z2_arrive(s, js):
        for j in js:
            for d in range(2):
                z2_copy(d, s, j).wait_recv()
                if s < 3:
                    go(z2_copy(d, s + 1, j))

    other = 1 - y_lo
    TASKS = (("u0", y_lo, 1), ("u1", y_lo, 1), ("u2", y_lo, 1), ("v", other, 1), ("u3", 0, 2), ("u4", 0, 2))

    def geometry(t):
        name, h, nh = TASKS[t]
        r0, n = UNITS[name]
        mine = pl.multiple_of(r0 + c * (n // 2), 16)
        theirs = pl.multiple_of(r0 + (1 - c) * (n // 2), 16)
        return h, nh, r0, n, mine, theirs

    def quarter(t, q):
        h, nh, r0, n, mine, theirs = geometry(t)
        return pl.multiple_of(mine + q * (n // 8), 16), n // 8

    def s1(t):
        h, nh, r0, n, mine, theirs = geometry(t)
        for k in range(nh):
            pbuf[h + k, r0:r0 + n] = jnp.dot(ht[r0:r0 + n, :], z1[h + k], preferred_element_type=F32)
        go(k_copy(t, theirs))

    def k_copy(t, start):
        h, nh, r0, n, mine, theirs = geometry(t)
        return rcopy(
            pbuf.at[pl.ds(h, nh), pl.ds(start, n // 2)], xbuf.at[pl.ds(h, nh), pl.ds(start, n // 2)],
            ks.at[t], kr.at[t], sib,
        )

    def rs_copy(t, d, q):
        h, nh = TASKS[t][1:]
        start, size = quarter(t, q)
        return rcopy(
            rss.at[pl.ds(h, nh), pl.ds(start, size)], rsr.at[d, pl.ds(h, nh), pl.ds(start, size)],
            rs_s.at[t, d], rs_r.at[t, d], xdev[d],
        )

    def ag_copy(t, d, q):
        h, nh = TASKS[t][1:]
        start, size = quarter(t, q)
        part = y.at[pl.ds(h, nh), pl.ds(start, size)]
        return rcopy(part, part, ag_s.at[t, d], ag_r.at[t, d], xdev[d])

    def f_copy(t, start):
        h, nh, r0, n, mine, theirs = geometry(t)
        part = y.at[pl.ds(h, nh), pl.ds(start, n // 2)]
        return rcopy(part, part, fs.at[t], fr.at[t], sib)

    def s2(t):
        h, nh, r0, n, mine, theirs = geometry(t)
        k_copy(t, mine).wait_recv()
        for k in range(nh):
            v = pbuf[h + k, pl.ds(mine, n // 2)] + xbuf[h + k, pl.ds(mine, n // 2)]
            pbuf[h + k, pl.ds(mine, n // 2)] = v
            rss[h + k, pl.ds(mine, n // 2)] = v.astype(BF)
        for d in (1, 0, 2):
            go(rs_copy(t, d, lax.rem(x + d + 1, 4)))

    def s3(t):
        h, nh = TASKS[t][1:]
        start, size = quarter(t, x)
        for d in range(3):
            rs_copy(t, d, x).wait_recv()
        for k in range(nh):
            v = pbuf[h + k, pl.ds(start, size)]
            for d in range(3):
                v = v + rsr[d, h + k, pl.ds(start, size)].astype(F32)
            y[h + k, pl.ds(start, size)] = v.astype(BF)
        for d in (1, 0, 2):
            go(ag_copy(t, d, x))

    def s4(t):
        h, nh, r0, n, mine, theirs = geometry(t)
        for d in range(3):
            ag_copy(t, d, lax.rem(x + 3 - d, 4)).wait_recv()
        go(f_copy(t, mine))

    def s5(t):
        h, nh, r0, n, mine, theirs = geometry(t)
        f_copy(t, theirs).wait_recv()

    U0, U1, U2, V, U3, U4 = range(6)
    s1(U0)
    h_arrive(0, 0)
    s2(U0)
    h_arrive(0, 1)
    h_arrive(0, 2)
    h_arrive(0, 3)
    s1(U1)
    s3(U0)
    h_arrive(1, 0)
    s2(U1)
    h_arrive(1, 1)
    h_arrive(1, 2)
    s4(U0)
    h_arrive(1, 3)
    s1(U2)
    s3(U1)
    h_arrive(2, 0)
    s2(U2)
    for d in range(2):
        z1_copy(d, other).wait_recv()
    s1(V)
    h_arrive(2, 1)
    s2(V)
    s4(U1)
    h_arrive(2, 2)
    h_arrive(2, 3)
    z2_start((0, 1))
    s1(U3)
    s3(U2)
    h_last(0)
    h_last(1)
    s2(U3)
    s1(U4)
    s3(V)
    s2(U4)
    s4(U2)
    z2_arrive(0, (0, 1))
    z2_start((2, 3))
    s3(U3)
    s4(V)
    s3(U4)
    z2_arrive(1, (0, 1))
    z2_arrive(0, (2, 3))
    s4(U3)
    s4(U4)
    for t in range(6):
        s5(t)

    def block_of(d):
        t = lax.rem(y_pos + d + 8, 8)
        return lax.rem(t, 2) * 4 + t // 2

    def c_chunk(j):
        rows = pl.ds(j * 256, 256)
        left = jnp.concatenate([z2[s, rows] for s in range(8)], axis=1)
        for h in range(2):
            part = jnp.dot(left, y[h], preferred_element_type=F32)
            for b in range(4):
                cpart[h * 4 + b, rows] = part[:, b * 128:(b + 1) * 128]

    def c_copy(d, t, j):
        start, size = j * 256, 256
        if t == 0:
            start, size = start + d * 128, 128
        return rcopy(
            csend.at[d, t, pl.ds(start, size)], crecv.at[d, t, pl.ds(start, size)],
            cs.at[d, t, j], cr.at[d, t, j], ydev[d],
        )

    def c_step(t, j):
        for d in range(2):
            b = block_of((4 - t) * (1 - 2 * d))
            mine = pl.ds(j * 256 + d * 128, 128)
            rest = pl.ds(j * 256 + (1 - d) * 128, 128)
            full = pl.ds(j * 256, 256)
            if t == 0:
                csend[d, t, mine] = cpart[b, mine].astype(BF)
            else:
                c_copy(d, t - 1, j).wait_recv()
                if t == 1:
                    csend[d, t, mine] = (cpart[b, mine] + crecv[d, 0, mine].astype(F32)).astype(BF)
                    csend[d, t, rest] = cpart[b, rest].astype(BF)
                else:
                    csend[d, t, full] = (cpart[b, full] + crecv[d, t - 1, full].astype(F32)).astype(BF)
            go(c_copy(d, t, j))

    def c_last(j):
        full = pl.ds(j * 256, 256)
        v = cpart[block_of(0), full]
        for d in range(2):
            c_copy(d, 3, j).wait_recv()
            v = v + crecv[d, 3, full].astype(F32)
        o_ref[full, :] = v.astype(BF)

    z2_arrive(2, (0, 1))
    z2_arrive(1, (2, 3))
    z2_arrive(3, (0, 1))
    c_chunk(0)
    c_step(0, 0)
    c_chunk(1)
    c_step(0, 1)
    z2_arrive(2, (2, 3))
    c_step(1, 0)
    c_step(1, 1)
    z2_arrive(3, (2, 3))
    c_chunk(2)
    c_step(0, 2)
    c_chunk(3)
    c_step(0, 3)
    c_step(2, 0)
    c_step(2, 1)
    c_step(1, 2)
    c_step(1, 3)
    c_step(3, 0)
    c_step(3, 1)
    c_step(2, 2)
    c_step(2, 3)
    c_last(0)
    c_last(1)
    c_step(3, 2)
    c_step(3, 3)
    c_last(2)
    c_last(3)
    for cp in pending:
        cp.wait_send()


def local(hamiltonian, inv_root, h_pattern, z_pattern):
    dma = pltpu.SemaphoreType.DMA
    smem = pl.BlockSpec(memory_space=pltpu.SMEM)
    vmem = pl.BlockSpec(memory_space=pltpu.VMEM)
    return pl.pallas_call(
        body,
        out_shape=jax.ShapeDtypeStruct((1024, 128), BF),
        in_specs=[smem, smem, vmem, vmem],
        out_specs=vmem,
        scratch_shapes=[
            pltpu.VMEM((1024, 1024), BF),
            pltpu.VMEM((2, 1024, 512), BF),
            pltpu.VMEM((8, 1024, 128), BF),
            pltpu.VMEM((2, 1024, 512), BF),
            pltpu.VMEM((2, 1024, 512), F32),
            pltpu.VMEM((2, 1024, 512), F32),
            pltpu.VMEM((2, 1024, 512), BF),
            pltpu.VMEM((3, 2, 1024, 512), BF),
            pltpu.VMEM((8, 1024, 128), F32),
            pltpu.VMEM((2, 4, 1024, 128), BF),
            pltpu.VMEM((2, 4, 1024, 128), BF),
            dma((2, 4, 4)), dma((2, 4, 4)),
            dma((2,)), dma((2,)),
            dma((2, 4, 4)), dma((2, 4, 4)),
            dma((6,)), dma((6,)),
            dma((6, 3)), dma((6, 3)),
            dma((6, 3)), dma((6, 3)),
            dma((6,)), dma((6,)),
            dma((2, 4, 4)), dma((2, 4, 4)),
        ],
        compiler_params=pltpu.CompilerParams(
            collective_id=0, has_side_effects=True, vmem_limit_bytes=56 * 2**20
        ),
        cost_estimate=pl.CostEstimate(flops=4 * 1024**3, bytes_accessed=3 * 2**19, transcendentals=0),
    )(h_pattern, z_pattern, hamiltonian, inv_root)


def solution(mesh):
    return jax.shard_map(
        local,
        mesh=mesh,
        in_specs=(P("row", ("col", "layer")), P("row", "col"), P(), P()),
        out_specs=P("row", ("col", "layer")),
        check_vma=False,
    )
```

time: 366 us -> 90.5 us (0.25)
  waiting for transfers between devices: 246 us -> 0 us
  Pallas kernels: 0 us -> 88.7 us
  blocking collectives: 85.9 us -> 0 us
  matrix products: 16.5 us -> 0 us
  between operations: 13.2 us -> 0.01 us
    all_gather x4 -> x0, waiting for transfers between devices: 193 us -> none  [the longest x1 84.6 us: local(): h_whole = lax.all_gather(h_local, 'col', axis=1, tiled=True)]
    pallas_call x0 -> x1, Pallas kernels: none -> 88.7 us  [local(): pl.pallas_call(body, out_shape=jax.ShapeDtypeStruct((1024, 128), BF), in_...]
    psum x1 -> x0, blocking collectives: 85.9 us -> none  [local(): summed = lax.psum(partial_y, 'layer')]
    reduce_scatter x1 -> x0, waiting for transfers between devices: 52.5 us -> none  [local(): lax.psum_scatter(partial_c, 'layer', scatter_dimension=1, tiled=True)]
    dot_general x6 -> x0, matrix products: 16.5 us -> none  [the longest x2 11.7 us: accumulate(): return jnp.dot(left, right, preferred_element_type=jnp.float32)]
  transfers between devices with their start and end apart: 5 -> 0, of which waited for: 5 -> 0; matrix products, arithmetic and copies ran while one was open for 2% -> 0% of each run, Pallas kernels for 0% -> 0%
where the time goes in v1:
time: 90.5 us; the launch traced here: 90.4 us
  Pallas kernels  88.7 us (98%)
  local copies, waits for them, and re-layouts  1.67 us (2%)
    pallas_call x1, Pallas kernels, local(): pl.pallas_call(body, out_shape=jax.ShapeDtypeStruct((1024, 128), BF), in_...  88.7 us

profile of v1, /device:TPU:1, one launch (start us, length us, event | category | flops | bytes accessed | tf_op | source)
XLA Modules:
  0.0 90.4 jit_solution(16366158808801649914)
XLA Ops:
  0.0 88.7 %shard_map.46 = bf16[1024,128]{1,0:T(8,128)(2,1)} custom-call(s32[32,32]{1,0:T(8,128)} %hp.1, s32[32,32]{1,0:T(8,128)} %zp.1, bf16[1024,128]{1,0:T(8,128)(2,1)} %h_ref.1, bf16[1024,512]{1,0:T(8,128)(2,1)} %z_ref.1), custom_call_target="tpu_custom_call" | custom-call | flops 4294967296 | bytes 1572864 | tf_op jit(solution)/shard_map/pallas_call | solution.py:334
  88.7 1.7 %copy.6 = bf16[1024,128]{1,0:T(8,128)(2,1)} copy(bf16[1024,128]{1,0:T(8,128)(2,1)} %shard_map.46) | data formatting | bytes 524288

commit v2 on v1

v2 whole, which is shorter than its diff:
```python
import functools
import jax
import jax.numpy as jnp
from jax import lax
from jax.experimental import pallas as pl
from jax.experimental.pallas import tpu as pltpu
from jax.sharding import PartitionSpec as P

BS = 256
BF = jnp.bfloat16
F32 = jnp.float32
MESH = pl.DeviceIdType.MESH

SRC = ((0, 1, 3, 5), (0, 2, 4, 6))
DST = ((1, 3, 5, 7), (2, 4, 6, 7))

TASKS = ((0, 128, 0, 2), (128, 256, 0, 2), (0, 384, 2, 1), (384, 256, 0, 3), (0, 640, 3, 1), (640, 256, 0, 4), (896, 128, 0, 4))


def body(hp, zp, h_hbm, z_hbm, o_hbm, h_ref, z_ref, o_ref, ht, z1, z2, y, pbuf, xbuf, rss, rsr, cpart, csend, crecv,
         io, oo, hs, hr, z1s, z1r, z2s, z2r, ks, kr, rs_s, rs_r, ag_s, ag_r, fs, fr, cs, cr):
    row = lax.axis_index("row")
    col = lax.axis_index("col")
    layer = lax.axis_index("layer")
    x, c = row // 2, lax.rem(row, 2)
    y_lo, z = col // 8, lax.rem(col, 8)
    y_pos = layer * 2 + y_lo

    def at_z(d):
        return {"col": y_lo * 8 + lax.rem(z + d + 8, 8)}

    def at_y(d):
        t = lax.rem(y_pos + d + 8, 8)
        return {"col": lax.rem(t, 2) * 8 + z, "layer": t // 2}

    def at_x(d):
        return {"row": lax.rem(x + d + 4, 4) * 2 + c}

    zdev = (at_z(1), at_z(-1))
    ydev = (at_y(1), at_y(-1))
    xdev = (at_x(1), at_x(2), at_x(3))
    sib = {"row": x * 2 + 1 - c}

    loads = [pltpu.make_async_copy(h_hbm, h_ref, io.at[0]), pltpu.make_async_copy(z_hbm, z_ref, io.at[1])]
    for cp in loads:
        cp.start()
    barrier = pltpu.get_barrier_semaphore()
    for d in (*zdev, *ydev, *xdev, sib):
        pl.semaphore_signal(barrier, inc=1, device_id=d, device_id_type=MESH)

    pending = []

    def rcopy(src, dst, s, r, dev):
        return pltpu.make_async_remote_copy(
            src_ref=src, dst_ref=dst, send_sem=s, recv_sem=r, device_id=dev, device_id_type=MESH
        )

    def go(cp):
        cp.start()
        pending.append(cp)

    loads[0].wait()
    for i in range(4):
        p = hp[row * 4 + i, col * 2 + layer // 2]
        keep = jnp.where(p > 0, 1.0, 0.0).astype(F32)
        blk = h_ref[i * BS:(i + 1) * BS, :].astype(F32) * keep
        ht[0:128, i * BS:(i + 1) * BS] = blk.T.astype(BF)

    pl.semaphore_wait(barrier, 8)

    def h_copy(d, s, j):
        j = j if d == 0 else 3 - j
        return rcopy(
            ht.at[pl.ds(SRC[d][s] * 128 + j * 32, 32)], ht.at[pl.ds(DST[d][s] * 128 + j * 32, 32)],
            hs.at[d, s, j], hr.at[d, s, j], zdev[d],
        )

    for j in range(4):
        for d in range(2):
            go(h_copy(d, 0, j))

    def z1_copy(k, d):
        rows = pl.ds(d * 512, 512)
        return rcopy(z1.at[k, rows], z1.at[2 + k, rows], z1s.at[k, d], z1r.at[k, d], ydev[d])

    loads[1].wait()
    for k in range(2):
        for i in range(4):
            p = zp[row * 4 + i, col * 2 + k]
            keep = jnp.where(p > 0, 1.0, 0.0).astype(F32)
            blk = z_ref[i * BS:(i + 1) * BS, k * BS:(k + 1) * BS].astype(F32) * keep
            z1[k, i * BS:(i + 1) * BS, :] = blk.astype(BF)
        for d in range(2):
            go(z1_copy(k, d))
    z2[0] = z1[layer // 2, :, pl.ds(pl.multiple_of(lax.rem(layer, 2) * 128, 128), 128)]

    def z2_copy(d, s, j):
        start, size = j * 256, 256
        if s == 3:
            start, size = start + d * 128, 128
        return rcopy(
            z2.at[SRC[d][s], pl.ds(start, size)], z2.at[DST[d][s], pl.ds(start, size)],
            z2s.at[d, s, j], z2r.at[d, s, j], zdev[d],
        )

    def h_arrive(s, j):
        for d in range(2):
            h_copy(d, s, j).wait_recv()
            if s < 2 or (s == 2 and j < 2):
                go(h_copy(d, s + 1, j))

    def h_last(j):
        for d in range(2):
            h_copy(d, 3, j).wait_recv()

    def z2_start(js):
        for j in js:
            for d in range(2):
                go(z2_copy(d, 0, j))

    def z2_arrive(s, js):
        for j in js:
            for d in range(2):
                z2_copy(d, s, j).wait_recv()
                if s < 3:
                    go(z2_copy(d, s + 1, j))

    def geometry(t):
        r0, n, h, nh = TASKS[t]
        mine = pl.multiple_of(r0 + c * (n // 2), 16)
        theirs = pl.multiple_of(r0 + (1 - c) * (n // 2), 16)
        return h, nh, r0, n, mine, theirs

    def quarter(t, q):
        h, nh, r0, n, mine, theirs = geometry(t)
        return pl.multiple_of(mine + q * (n // 8), 16), n // 8

    def s1(t):
        h, nh, r0, n, mine, theirs = geometry(t)
        for k in range(nh):
            pbuf[h + k, r0:r0 + n] = jnp.dot(ht[r0:r0 + n, :], z1[h + k], preferred_element_type=F32)
        go(k_copy(t, theirs))

    def k_copy(t, start):
        h, nh, r0, n, mine, theirs = geometry(t)
        return rcopy(
            pbuf.at[pl.ds(h, nh), pl.ds(start, n // 2)], xbuf.at[pl.ds(h, nh), pl.ds(start, n // 2)],
            ks.at[t], kr.at[t], sib,
        )

    def rs_copy(t, d, q):
        h, nh = TASKS[t][2:]
        start, size = quarter(t, q)
        return rcopy(
            rss.at[pl.ds(h, nh), pl.ds(start, size)], rsr.at[d, pl.ds(h, nh), pl.ds(start, size)],
            rs_s.at[t, d], rs_r.at[t, d], xdev[d],
        )

    def ag_copy(t, d, q):
        h, nh = TASKS[t][2:]
        start, size = quarter(t, q)
        part = y.at[pl.ds(h, nh), pl.ds(start, size)]
        return rcopy(part, part, ag_s.at[t, d], ag_r.at[t, d], xdev[d])

    def f_copy(t, start):
        h, nh, r0, n, mine, theirs = geometry(t)
        part = y.at[pl.ds(h, nh), pl.ds(start, n // 2)]
        return rcopy(part, part, fs.at[t], fr.at[t], sib)

    def s2(t):
        h, nh, r0, n, mine, theirs = geometry(t)
        k_copy(t, mine).wait_recv()
        for k in range(nh):
            v = pbuf[h + k, pl.ds(mine, n // 2)] + xbuf[h + k, pl.ds(mine, n // 2)]
            pbuf[h + k, pl.ds(mine, n // 2)] = v
            rss[h + k, pl.ds(mine, n // 2)] = v.astype(BF)
        for d in (1, 0, 2):
            go(rs_copy(t, d, lax.rem(x + d + 1, 4)))

    def s3(t):
        h, nh = TASKS[t][2:]
        start, size = quarter(t, x)
        for d in range(3):
            rs_copy(t, d, x).wait_recv()
        for k in range(nh):
            v = pbuf[h + k, pl.ds(start, size)]
            for d in range(3):
                v = v + rsr[d, h + k, pl.ds(start, size)].astype(F32)
            y[h + k, pl.ds(start, size)] = v.astype(BF)
        for d in (1, 0, 2):
            go(ag_copy(t, d, x))

    def s4(t):
        h, nh, r0, n, mine, theirs = geometry(t)
        for d in range(3):
            ag_copy(t, d, lax.rem(x + 3 - d, 4)).wait_recv()
        go(f_copy(t, mine))

    def s5(t):
        h, nh, r0, n, mine, theirs = geometry(t)
        f_copy(t, theirs).wait_recv()

    def z1_arrive(k):
        for d in range(2):
            z1_copy(k, d).wait_recv()

    s1(0)
    h_arrive(0, 0)
    s2(0)
    h_arrive(0, 1)
    h_arrive(0, 2)
    h_arrive(0, 3)
    s3(0)
    s1(1)
    z1_arrive(0)
    s1(2)
    h_arrive(1, 0)
    h_arrive(1, 1)
    s2(1)
    s2(2)
    h_arrive(1, 2)
    s4(0)
    h_arrive(1, 3)
    s1(3)
    z1_arrive(1)
    s1(4)
    h_arrive(2, 0)
    s3(1)
    h_arrive(2, 1)
    s2(3)
    s2(4)
    s3(2)
    h_arrive(2, 2)
    z2_start((0, 1, 2, 3,))
    h_arrive(2, 3)
    s1(5)
    h_last(0)
    s2(5)
    h_last(1)
    s1(6)
    s3(3)
    z2_arrive(0, (0,))
    s3(4)
    s2(6)
    z2_arrive(0, (1,))
    z2_arrive(0, (2,))
    z2_arrive(0, (3,))
    s4(1)
    s4(2)
    z2_arrive(1, (0,))
    s3(5)
    z2_arrive(1, (1,))
    s3(6)
    z2_arrive(1, (2,))
    z2_arrive(1, (3,))
    s4(3)
    s4(4)
    z2_arrive(2, (0,))
    z2_arrive(2, (1,))
    z2_arrive(2, (2,))
    z2_arrive(2, (3,))
    s4(5)
    s4(6)
    z2_arrive(3, (0,))
    z2_arrive(3, (1,))
    s5(0)
    s5(1)
    s5(2)
    s5(3)
    s5(4)
    s5(5)
    s5(6)

    def block_of(d):
        t = lax.rem(y_pos + d + 8, 8)
        return (d % 2) * 4 + t // 2

    def c_chunk(j):
        rows = pl.ds(j * 256, 256)
        left = jnp.concatenate([z2[s, rows] for s in range(8)], axis=1)
        for q in range(4):
            part = jnp.dot(left, y[q], preferred_element_type=F32)
            for b in range(2):
                cpart[q * 2 + b, rows] = part[:, b * 128:(b + 1) * 128]

    def c_copy(d, t, j):
        start, size = j * 256, 256
        if t in (0, 1, 4):
            start, size = start + (1 - d if t == 4 else d) * 128, 128
        slot = 1 if t == 4 else t
        return rcopy(
            csend.at[d, slot, pl.ds(start, size)], crecv.at[d, slot, pl.ds(start, size)],
            cs.at[d, t, j], cr.at[d, t, j], ydev[d],
        )

    def c_start(j):
        for d in range(2):
            for t, half in ((0, d), (4, 1 - d)):
                rows = pl.ds(j * 256 + half * 128, 128)
                hop = 4 if t == 0 else 3
                csend[d, t // 4, rows] = cpart[block_of(hop * (1 - 2 * d)), rows].astype(BF)
                go(c_copy(d, t, j))

    def c_step(t, j):
        for d in range(2):
            b = block_of((4 - t) * (1 - 2 * d))
            rows = pl.ds(j * 256 + d * 128, 128) if t == 1 else pl.ds(j * 256, 256)
            c_copy(d, t - 1, j).wait_recv()
            if t == 2:
                c_copy(d, 4, j).wait_recv()
            csend[d, t, rows] = (cpart[b, rows] + crecv[d, t - 1, rows].astype(F32)).astype(BF)
            go(c_copy(d, t, j))

    stores = []

    def c_last(j):
        full = pl.ds(j * 256, 256)
        v = cpart[block_of(0), full]
        for d in range(2):
            c_copy(d, 3, j).wait_recv()
            v = v + crecv[d, 3, full].astype(F32)
        o_ref[full, :] = v.astype(BF)
        cp = pltpu.make_async_copy(o_ref.at[full], o_hbm.at[full], oo.at[j])
        cp.start()
        stores.append(cp)

    c_chunk(0)
    c_start(0)
    c_chunk(1)
    c_start(1)
    z2_arrive(3, (2,))
    c_chunk(2)
    c_start(2)
    z2_arrive(3, (3,))
    c_chunk(3)
    c_start(3)
    c_step(1, 0)
    c_step(1, 1)
    c_step(1, 2)
    c_step(1, 3)
    c_step(2, 0)
    c_step(2, 1)
    c_step(2, 2)
    c_step(2, 3)
    c_step(3, 0)
    c_step(3, 1)
    c_step(3, 2)
    c_step(3, 3)
    c_last(0)
    c_last(1)
    c_last(2)
    c_last(3)
    for cp in stores:
        cp.wait()
    for cp in pending:
        cp.wait_send()


def local(hamiltonian, inv_root, h_pattern, z_pattern):
    dma = pltpu.SemaphoreType.DMA
    smem = pl.BlockSpec(memory_space=pltpu.SMEM)
    hbm = pl.BlockSpec(memory_space=pl.ANY)
    return pl.pallas_call(
        body,
        out_shape=jax.ShapeDtypeStruct((1024, 128), BF),
        in_specs=[smem, smem, hbm, hbm],
        out_specs=hbm,
        scratch_shapes=[
            pltpu.VMEM((1024, 128), BF),
            pltpu.VMEM((1024, 512), BF),
            pltpu.VMEM((1024, 128), BF),
            pltpu.VMEM((1024, 1024), BF),
            pltpu.VMEM((4, 1024, 256), BF),
            pltpu.VMEM((8, 1024, 128), BF),
            pltpu.VMEM((4, 1024, 256), BF),
            pltpu.VMEM((4, 1024, 256), F32),
            pltpu.VMEM((4, 1024, 256), F32),
            pltpu.VMEM((4, 1024, 256), BF),
            pltpu.VMEM((3, 4, 1024, 256), BF),
            pltpu.VMEM((8, 1024, 128), F32),
            pltpu.VMEM((2, 4, 1024, 128), BF),
            pltpu.VMEM((2, 4, 1024, 128), BF),
            dma((2,)), dma((4,)),
            dma((2, 4, 4)), dma((2, 4, 4)),
            dma((2, 2)), dma((2, 2)),
            dma((2, 4, 4)), dma((2, 4, 4)),
            dma((7,)), dma((7,)),
            dma((7, 3)), dma((7, 3)),
            dma((7, 3)), dma((7, 3)),
            dma((7,)), dma((7,)),
            dma((2, 5, 4)), dma((2, 5, 4)),
        ],
        compiler_params=pltpu.CompilerParams(
            collective_id=0, has_side_effects=True, vmem_limit_bytes=56 * 2**20
        ),
        cost_estimate=pl.CostEstimate(flops=4 * 1024**3, bytes_accessed=3 * 2**19, transcendentals=0),
    )(h_pattern, z_pattern, hamiltonian, inv_root)


def solution(mesh):
    return jax.shard_map(
        local,
        mesh=mesh,
        in_specs=(P("row", ("col", "layer")), P("row", "col"), P(), P()),
        out_specs=P("row", ("col", "layer")),
        check_vma=False,
    )
```

time: 90.5 us -> 83.8 us (0.926)
  Pallas kernels: 88.7 us -> 81.8 us
    pallas_call x1, Pallas kernels: 88.7 us -> 81.8 us  [local(): pl.pallas_call(body, out_shape=jax.ShapeDtypeStruct((1024, 128), BF), in_...]
where the time goes in v2:
time: 83.8 us; the launch traced here: 83.5 us
  Pallas kernels  81.8 us (98%)
  local copies, waits for them, and re-layouts  1.67 us (2%)
    pallas_call x1, Pallas kernels, local(): pl.pallas_call(body, out_shape=jax.ShapeDtypeStruct((1024, 128), BF), in_...  81.8 us

profile of v2, /device:TPU:1, one launch (start us, length us, event | category | flops | bytes accessed | tf_op | source)
XLA Modules:
  0.0 83.5 jit_solution(16425486359953120821)
XLA Ops:
  0.0 81.8 %shard_map.46 = bf16[1024,128]{1,0:T(8,128)(2,1)} custom-call(s32[32,32]{1,0:T(8,128)} %hp.1, s32[32,32]{1,0:T(8,128)} %zp.1, bf16[1024,128]{1,0:T(8,128)(2,1)} %h_hbm.1, bf16[1024,512]{1,0:T(8,128)(2,1)} %z_hbm.1), custom_call_target="tpu_custom_call" | custom-call | flops 4294967296 | bytes 1572864 | tf_op jit(solution)/shard_map/pallas_call | solution.py:363
  81.8 1.7 %copy.6 = bf16[1024,128]{1,0:T(8,128)(2,1)} copy(bf16[1024,128]{1,0:T(8,128)(2,1)} %shard_map.46) | data formatting | bytes 524288

commit v3 on v2

--- a/solution.py
+++ b/solution.py
@@ -15,6 +15,8 @@
 DST = ((1, 3, 5, 7), (2, 4, 6, 7))
 
 TASKS = ((0, 128, 0, 2), (128, 256, 0, 2), (0, 384, 2, 1), (384, 256, 0, 3), (0, 640, 3, 1), (640, 256, 0, 4), (896, 128, 0, 4))
+
+RING = (1, 2, 3, 4)
 
 
 def body(hp, zp, h_hbm, z_hbm, o_hbm, h_ref, z_ref, o_ref, ht, z1, z2, y, pbuf, xbuf, rss, rsr, cpart, csend, crecv,
@@ -48,16 +50,16 @@
     for d in (*zdev, *ydev, *xdev, sib):
         pl.semaphore_signal(barrier, inc=1, device_id=d, device_id_type=MESH)
 
-    pending = []
-
     def rcopy(src, dst, s, r, dev):
         return pltpu.make_async_remote_copy(
             src_ref=src, dst_ref=dst, send_sem=s, recv_sem=r, device_id=dev, device_id_type=MESH
         )
 
+    def await_all(ref, sem):
+        pltpu.make_async_copy(ref, ref, sem).wait()
+
     def go(cp):
         cp.start()
-        pending.append(cp)
 
     loads[0].wait()
     for i in range(4):
@@ -72,7 +74,7 @@
         j = j if d == 0 else 3 - j
         return rcopy(
             ht.at[pl.ds(SRC[d][s] * 128 + j * 32, 32)], ht.at[pl.ds(DST[d][s] * 128 + j * 32, 32)],
-            hs.at[d, s, j], hr.at[d, s, j], zdev[d],
+            hs.at[0], hr.at[d, s, j], zdev[d],
         )
 
     for j in range(4):
@@ -81,7 +83,7 @@
 
     def z1_copy(k, d):
         rows = pl.ds(d * 512, 512)
-        return rcopy(z1.at[k, rows], z1.at[2 + k, rows], z1s.at[k, d], z1r.at[k, d], ydev[d])
+        return rcopy(z1.at[k, rows], z1.at[2 + k, rows], z1s.at[0], z1r.at[k, d], ydev[d])
 
     loads[1].wait()
     for k in range(2):
@@ -100,7 +102,7 @@
             start, size = start + d * 128, 128
         return rcopy(
             z2.at[SRC[d][s], pl.ds(start, size)], z2.at[DST[d][s], pl.ds(start, size)],
-            z2s.at[d, s, j], z2r.at[d, s, j], zdev[d],
+            z2s.at[0], z2r.at[d, s, j], zdev[d],
         )
 
     def h_arrive(s, j):
@@ -145,7 +147,7 @@
         h, nh, r0, n, mine, theirs = geometry(t)
         return rcopy(
             pbuf.at[pl.ds(h, nh), pl.ds(start, n // 2)], xbuf.at[pl.ds(h, nh), pl.ds(start, n // 2)],
-            ks.at[t], kr.at[t], sib,
+            ks.at[0], kr.at[t], sib,
         )
 
     def rs_copy(t, d, q):
@@ -153,19 +155,19 @@
         start, size = quarter(t, q)
         return rcopy(
             rss.at[pl.ds(h, nh), pl.ds(start, size)], rsr.at[d, pl.ds(h, nh), pl.ds(start, size)],
-            rs_s.at[t, d], rs_r.at[t, d], xdev[d],
+            rs_s.at[0], rs_r.at[t, 0], xdev[d],
         )
 
     def ag_copy(t, d, q):
         h, nh = TASKS[t][2:]
         start, size = quarter(t, q)
         part = y.at[pl.ds(h, nh), pl.ds(start, size)]
-        return rcopy(part, part, ag_s.at[t, d], ag_r.at[t, d], xdev[d])
+        return rcopy(part, part, ag_s.at[0], ag_r.at[t, 0], xdev[d])
 
     def f_copy(t, start):
         h, nh, r0, n, mine, theirs = geometry(t)
         part = y.at[pl.ds(h, nh), pl.ds(start, n // 2)]
-        return rcopy(part, part, fs.at[t], fr.at[t], sib)
+        return rcopy(part, part, fs.at[0], fr.at[t], sib)
 
     def s2(t):
         h, nh, r0, n, mine, theirs = geometry(t)
@@ -174,31 +176,81 @@
             v = pbuf[h + k, pl.ds(mine, n // 2)] + xbuf[h + k, pl.ds(mine, n // 2)]
             pbuf[h + k, pl.ds(mine, n // 2)] = v
             rss[h + k, pl.ds(mine, n // 2)] = v.astype(BF)
+        if t in RING:
+            for i in (0, 3, 1, 4):
+                go(ring_rs(t, i, x + 2 if i % 3 == 0 else x + sign(i)))
+            return
         for d in (1, 0, 2):
             go(rs_copy(t, d, lax.rem(x + d + 1, 4)))
 
+    def sign(i):
+        return 1 if i < 3 else -1
+
+    def half_rows(t, q, second):
+        start, size = quarter(t, lax.rem(q + 4, 4))
+        low = size // 32 * 16
+        return pl.ds(start + low, size - low) if second else pl.ds(start, low)
+
+    def ring_rs(t, i, q):
+        h, nh = TASKS[t][2:]
+        rows = half_rows(t, q, (i % 3 == 1) == (i < 3))
+        d = 0 if i < 3 else 2
+        return rcopy(
+            rss.at[pl.ds(h, nh), rows], rsr.at[d, pl.ds(h, nh), rows], rs_s.at[0], rs_r.at[t, {0: 1, 3: 2}.get(i, 0)], xdev[d]
+        )
+
+    def s6(t):
+        h, nh = TASKS[t][2:]
+        for i in (0, 3):
+            q = x + sign(i)
+            rows = half_rows(t, q, i == 3)
+            ring_rs(t, i, q).wait_recv()
+            for k in range(nh):
+                v = pbuf[h + k, rows] + rsr[0 if i == 0 else 2, h + k, rows].astype(F32)
+                rss[h + k, rows] = v.astype(BF)
+            go(ring_rs(t, i + 2, q))
+
+    def ring_ag(t, i, q):
+        h, nh = TASKS[t][2:]
+        start, size = quarter(t, lax.rem(q + 4, 4))
+        rows = pl.ds(start, size) if i < 2 else half_rows(t, q, i == 3)
+        part = y.at[pl.ds(h, nh), rows]
+        return rcopy(part, part, ag_s.at[0], ag_r.at[t, {0: 1, 1: 2}.get(i, 0)], xdev[i % 2 * 2])
+
+    def s7(t):
+        ring_ag(t, 0, x - 1).wait_recv()
+        go(ring_ag(t, 2, x - 1))
+        ring_ag(t, 1, x + 1).wait_recv()
+        go(ring_ag(t, 3, x + 1))
+
     def s3(t):
         h, nh = TASKS[t][2:]
         start, size = quarter(t, x)
-        for d in range(3):
-            rs_copy(t, d, x).wait_recv()
+        await_all(rsr.at[pl.ds(0, 2 if t in RING else 3), pl.ds(h, nh), pl.ds(start, size)], rs_r.at[t, 0])
         for k in range(nh):
             v = pbuf[h + k, pl.ds(start, size)]
-            for d in range(3):
+            for d in (0, 2) if t in RING else (0, 1, 2):
                 v = v + rsr[d, h + k, pl.ds(start, size)].astype(F32)
             y[h + k, pl.ds(start, size)] = v.astype(BF)
+        if t in RING:
+            for i in range(2):
+                go(ring_ag(t, i, x))
+            return
         for d in (1, 0, 2):
             go(ag_copy(t, d, x))
 
     def s4(t):
         h, nh, r0, n, mine, theirs = geometry(t)
-        for d in range(3):
-            ag_copy(t, d, lax.rem(x + 3 - d, 4)).wait_recv()
+        await_all(y.at[pl.ds(h, nh), pl.ds(mine, n // 8 * (1 if t in RING else 3))], ag_r.at[t, 0])
         go(f_copy(t, mine))
 
     def s5(t):
         h, nh, r0, n, mine, theirs = geometry(t)
         f_copy(t, theirs).wait_recv()
+
+    def z1_arrive(k):
+        for d in range(2):
+            z1_copy(k, d).wait_recv()
 
     def z1_arrive(k):
         for d in range(2):
@@ -215,34 +267,40 @@
     z1_arrive(0)
     s1(2)
     h_arrive(1, 0)
+    s2(1)
     h_arrive(1, 1)
-    s2(1)
     s2(2)
     h_arrive(1, 2)
     s4(0)
     h_arrive(1, 3)
     s1(3)
+    s6(1)
     z1_arrive(1)
     s1(4)
     h_arrive(2, 0)
-    s3(1)
+    s6(2)
+    s2(3)
     h_arrive(2, 1)
-    s2(3)
     s2(4)
-    s3(2)
     h_arrive(2, 2)
     z2_start((0, 1, 2, 3,))
+    s3(1)
+    s3(2)
     h_arrive(2, 3)
     s1(5)
+    s6(3)
     h_last(0)
     s2(5)
+    s6(4)
     h_last(1)
     s1(6)
+    s7(1)
+    s7(2)
+    z2_arrive(0, (0,))
     s3(3)
-    z2_arrive(0, (0,))
-    s3(4)
     s2(6)
     z2_arrive(0, (1,))
+    s3(4)
     z2_arrive(0, (2,))
     z2_arrive(0, (3,))
     s4(1)
@@ -250,6 +308,8 @@
     z2_arrive(1, (0,))
     s3(5)
     z2_arrive(1, (1,))
+    s7(3)
+    s7(4)
     s3(6)
     z2_arrive(1, (2,))
     z2_arrive(1, (3,))
@@ -290,7 +350,7 @@
         slot = 1 if t == 4 else t
         return rcopy(
             csend.at[d, slot, pl.ds(start, size)], crecv.at[d, slot, pl.ds(start, size)],
-            cs.at[d, t, j], cr.at[d, t, j], ydev[d],
+            cs.at[0], cr.at[d, t, j], ydev[d],
         )
 
     def c_start(j):
@@ -352,8 +412,14 @@
     c_last(3)
     for cp in stores:
         cp.wait()
-    for cp in pending:
-        cp.wait_send()
+    await_all(ht.at[pl.ds(0, 896)], hs.at[0])
+    await_all(z1.at[pl.ds(0, 2)], z1s.at[0])
+    await_all(z2.at[pl.ds(0, 7)], z2s.at[0])
+    await_all(pbuf.at[:, pl.ds(0, 512)], ks.at[0])
+    await_all(rss.at[:, pl.ds(0, 384)], rs_s.at[0])
+    await_all(y.at[:, pl.ds(0, 384)], ag_s.at[0])
+    await_all(y.at[:, pl.ds(0, 512)], fs.at[0])
+    await_all(z2.at[pl.ds(0, 7)], cs.at[0])
 
 
 def local(hamiltonian, inv_root, h_pattern, z_pattern):
@@ -381,14 +447,14 @@
             pltpu.VMEM((2, 4, 1024, 128), BF),
             pltpu.VMEM((2, 4, 1024, 128), BF),
             dma((2,)), dma((4,)),
-            dma((2, 4, 4)), dma((2, 4, 4)),
-            dma((2, 2)), dma((2, 2)),
-            dma((2, 4, 4)), dma((2, 4, 4)),
-            dma((7,)), dma((7,)),
-            dma((7, 3)), dma((7, 3)),
-            dma((7, 3)), dma((7, 3)),
-            dma((7,)), dma((7,)),
-            dma((2, 5, 4)), dma((2, 5, 4)),
+            dma((1,)), dma((2, 4, 4)),
+            dma((1,)), dma((2, 2)),
+            dma((1,)), dma((2, 4, 4)),
+            dma((1,)), dma((7,)),
+            dma((1,)), dma((7, 3)),
+            dma((1,)), dma((7, 3)),
+            dma((1,)), dma((7,)),
+            dma((1,)), dma((2, 5, 4)),
         ],
         compiler_params=pltpu.CompilerParams(
             collective_id=0, has_side_effects=True, vmem_limit_bytes=56 * 2**20

time: 83.8 us -> 80.9 us (0.965)
  Pallas kernels: 81.8 us -> 78.5 us
    pallas_call x1, Pallas kernels: 81.8 us -> 78.5 us  [local(): pl.pallas_call(body, out_shape=jax.ShapeDtypeStruct((1024, 128), BF), in_...]
where the time goes in v3:
time: 80.9 us; the launch traced here: 80.2 us
  Pallas kernels  78.5 us (97%)
  local copies, waits for them, and re-layouts  1.67 us (2%)
    pallas_call x1, Pallas kernels, local(): pl.pallas_call(body, out_shape=jax.ShapeDtypeStruct((1024, 128), BF), in_...  78.5 us
    unnamed x1, local copies, waits for them, and re-layouts  1.67 us

profile of v3, /device:TPU:1, one launch (start us, length us, event | category | flops | bytes accessed | tf_op | source)
XLA Modules:
  0.0 80.2 jit_solution(11355826998818553302)
XLA Ops:
  0.0 78.5 %shard_map.46 = bf16[1024,128]{1,0:T(8,128)(2,1)} custom-call(s32[32,32]{1,0:T(8,128)} %hp.1, s32[32,32]{1,0:T(8,128)} %zp.1, bf16[1024,128]{1,0:T(8,128)(2,1)} %h_hbm.1, bf16[1024,512]{1,0:T(8,128)(2,1)} %z_hbm.1), custom_call_target="tpu_custom_call" | custom-call | flops 4294967296 | bytes 1572864 | tf_op jit(solution)/shard_map/pallas_call | solution.py:429
  78.5 1.7 %copy.6 = bf16[1024,128]{1,0:T(8,128)(2,1)} copy(bf16[1024,128]{1,0:T(8,128)(2,1)} %shard_map.46) | data formatting | bytes 524288

commit v4 on v3

--- a/solution.py
+++ b/solution.py
@@ -71,10 +71,10 @@
     pl.semaphore_wait(barrier, 8)
 
     def h_copy(d, s, j):
-        j = j if d == 0 else 3 - j
+        k, j = j, j if d == 0 else 3 - j
         return rcopy(
             ht.at[pl.ds(SRC[d][s] * 128 + j * 32, 32)], ht.at[pl.ds(DST[d][s] * 128 + j * 32, 32)],
-            hs.at[0], hr.at[d, s, j], zdev[d],
+            hs.at[0], hr.at[s, k], zdev[d],
         )
 
     for j in range(4):
@@ -102,18 +102,17 @@
             start, size = start + d * 128, 128
         return rcopy(
             z2.at[SRC[d][s], pl.ds(start, size)], z2.at[DST[d][s], pl.ds(start, size)],
-            z2s.at[0], z2r.at[d, s, j], zdev[d],
+            z2s.at[0], z2r.at[s, j], zdev[d],
         )
 
     def h_arrive(s, j):
-        for d in range(2):
-            h_copy(d, s, j).wait_recv()
+        await_all(ht.at[pl.ds(0, 64)], hr.at[s, j])
+        for d in range(2):
             if s < 2 or (s == 2 and j < 2):
                 go(h_copy(d, s + 1, j))
 
     def h_last(j):
-        for d in range(2):
-            h_copy(d, 3, j).wait_recv()
+        await_all(ht.at[pl.ds(0, 64)], hr.at[3, j])
 
     def z2_start(js):
         for j in js:
@@ -122,8 +121,8 @@
 
     def z2_arrive(s, js):
         for j in js:
+            await_all(z2.at[0, pl.ds(0, 256 if s == 3 else 512)], z2r.at[s, j])
             for d in range(2):
-                z2_copy(d, s, j).wait_recv()
                 if s < 3:
                     go(z2_copy(d, s + 1, j))
 
@@ -155,14 +154,14 @@
         start, size = quarter(t, q)
         return rcopy(
             rss.at[pl.ds(h, nh), pl.ds(start, size)], rsr.at[d, pl.ds(h, nh), pl.ds(start, size)],
-            rs_s.at[0], rs_r.at[t, 0], xdev[d],
+            rs_s.at[0], rs_r.at[t], xdev[d],
         )
 
     def ag_copy(t, d, q):
         h, nh = TASKS[t][2:]
         start, size = quarter(t, q)
         part = y.at[pl.ds(h, nh), pl.ds(start, size)]
-        return rcopy(part, part, ag_s.at[0], ag_r.at[t, 0], xdev[d])
+        return rcopy(part, part, ag_s.at[0], ag_r.at[t], xdev[d])
 
     def f_copy(t, start):
         h, nh, r0, n, mine, theirs = geometry(t)
@@ -180,7 +179,7 @@
             for i in (0, 3, 1, 4):
                 go(ring_rs(t, i, x + 2 if i % 3 == 0 else x + sign(i)))
             return
-        for d in (1, 0, 2):
+        for d in (0, 2, 1):
             go(rs_copy(t, d, lax.rem(x + d + 1, 4)))
 
     def sign(i):
@@ -196,15 +195,15 @@
         rows = half_rows(t, q, (i % 3 == 1) == (i < 3))
         d = 0 if i < 3 else 2
         return rcopy(
-            rss.at[pl.ds(h, nh), rows], rsr.at[d, pl.ds(h, nh), rows], rs_s.at[0], rs_r.at[t, {0: 1, 3: 2}.get(i, 0)], xdev[d]
+            rss.at[pl.ds(h, nh), rows], rsr.at[d, pl.ds(h, nh), rows], rs_s.at[0], rs_r.at[7 + t if i % 3 == 0 else t], xdev[d]
         )
 
     def s6(t):
         h, nh = TASKS[t][2:]
+        await_all(rsr.at[0, pl.ds(h, nh), pl.ds(*quarter(t, x))], rs_r.at[7 + t])
         for i in (0, 3):
             q = x + sign(i)
             rows = half_rows(t, q, i == 3)
-            ring_rs(t, i, q).wait_recv()
             for k in range(nh):
                 v = pbuf[h + k, rows] + rsr[0 if i == 0 else 2, h + k, rows].astype(F32)
                 rss[h + k, rows] = v.astype(BF)
@@ -215,18 +214,18 @@
         start, size = quarter(t, lax.rem(q + 4, 4))
         rows = pl.ds(start, size) if i < 2 else half_rows(t, q, i == 3)
         part = y.at[pl.ds(h, nh), rows]
-        return rcopy(part, part, ag_s.at[0], ag_r.at[t, {0: 1, 1: 2}.get(i, 0)], xdev[i % 2 * 2])
+        return rcopy(part, part, ag_s.at[0], ag_r.at[7 + t if i < 2 else t], xdev[i % 2 * 2])
 
     def s7(t):
-        ring_ag(t, 0, x - 1).wait_recv()
+        h, nh, r0, n, mine, theirs = geometry(t)
+        await_all(y.at[pl.ds(h, nh), pl.ds(mine, n // 4)], ag_r.at[7 + t])
         go(ring_ag(t, 2, x - 1))
-        ring_ag(t, 1, x + 1).wait_recv()
         go(ring_ag(t, 3, x + 1))
 
     def s3(t):
         h, nh = TASKS[t][2:]
         start, size = quarter(t, x)
-        await_all(rsr.at[pl.ds(0, 2 if t in RING else 3), pl.ds(h, nh), pl.ds(start, size)], rs_r.at[t, 0])
+        await_all(rsr.at[pl.ds(0, 2 if t in RING else 3), pl.ds(h, nh), pl.ds(start, size)], rs_r.at[t])
         for k in range(nh):
             v = pbuf[h + k, pl.ds(start, size)]
             for d in (0, 2) if t in RING else (0, 1, 2):
@@ -236,12 +235,12 @@
             for i in range(2):
                 go(ring_ag(t, i, x))
             return
-        for d in (1, 0, 2):
+        for d in (0, 2, 1):
             go(ag_copy(t, d, x))
 
     def s4(t):
         h, nh, r0, n, mine, theirs = geometry(t)
-        await_all(y.at[pl.ds(h, nh), pl.ds(mine, n // 8 * (1 if t in RING else 3))], ag_r.at[t, 0])
+        await_all(y.at[pl.ds(h, nh), pl.ds(mine, n // 8 * (1 if t in RING else 3))], ag_r.at[t])
         go(f_copy(t, mine))
 
     def s5(t):
@@ -302,25 +301,25 @@
     z2_arrive(0, (1,))
     s3(4)
     z2_arrive(0, (2,))
+    s3(5)
     z2_arrive(0, (3,))
     s4(1)
     s4(2)
     z2_arrive(1, (0,))
-    s3(5)
-    z2_arrive(1, (1,))
     s7(3)
     s7(4)
     s3(6)
+    z2_arrive(1, (1,))
     z2_arrive(1, (2,))
     z2_arrive(1, (3,))
+    s4(5)
+    z2_arrive(2, (0,))
+    z2_arrive(2, (1,))
     s4(3)
     s4(4)
-    z2_arrive(2, (0,))
-    z2_arrive(2, (1,))
+    s4(6)
     z2_arrive(2, (2,))
     z2_arrive(2, (3,))
-    s4(5)
-    s4(6)
     z2_arrive(3, (0,))
     z2_arrive(3, (1,))
     s5(0)
@@ -350,7 +349,7 @@
         slot = 1 if t == 4 else t
         return rcopy(
             csend.at[d, slot, pl.ds(start, size)], crecv.at[d, slot, pl.ds(start, size)],
-            cs.at[0], cr.at[d, t, j], ydev[d],
+            cs.at[0], cr.at[t, j], ydev[d],
         )
 
     def c_start(j):
@@ -361,13 +360,16 @@
                 csend[d, t // 4, rows] = cpart[block_of(hop * (1 - 2 * d)), rows].astype(BF)
                 go(c_copy(d, t, j))
 
+    def c_wait(t, j):
+        await_all(crecv.at[0, 0, pl.ds(0, 512 if t in (2, 3) else 256)], cr.at[t, j])
+
     def c_step(t, j):
+        c_wait(t - 1, j)
+        if t == 2:
+            c_wait(4, j)
         for d in range(2):
             b = block_of((4 - t) * (1 - 2 * d))
             rows = pl.ds(j * 256 + d * 128, 128) if t == 1 else pl.ds(j * 256, 256)
-            c_copy(d, t - 1, j).wait_recv()
-            if t == 2:
-                c_copy(d, 4, j).wait_recv()
             csend[d, t, rows] = (cpart[b, rows] + crecv[d, t - 1, rows].astype(F32)).astype(BF)
             go(c_copy(d, t, j))
 
@@ -376,8 +378,8 @@
     def c_last(j):
         full = pl.ds(j * 256, 256)
         v = cpart[block_of(0), full]
-        for d in range(2):
-            c_copy(d, 3, j).wait_recv()
+        c_wait(3, j)
+        for d in range(2):
             v = v + crecv[d, 3, full].astype(F32)
         o_ref[full, :] = v.astype(BF)
         cp = pltpu.make_async_copy(o_ref.at[full], o_hbm.at[full], oo.at[j])
@@ -447,14 +449,14 @@
             pltpu.VMEM((2, 4, 1024, 128), BF),
             pltpu.VMEM((2, 4, 1024, 128), BF),
             dma((2,)), dma((4,)),
-            dma((1,)), dma((2, 4, 4)),
+            dma((1,)), dma((4, 4)),
             dma((1,)), dma((2, 2)),
-            dma((1,)), dma((2, 4, 4)),
+            dma((1,)), dma((4, 4)),
             dma((1,)), dma((7,)),
-            dma((1,)), dma((7, 3)),
-            dma((1,)), dma((7, 3)),
+            dma((1,)), dma((12,)),
+            dma((1,)), dma((12,)),
             dma((1,)), dma((7,)),
-            dma((1,)), dma((2, 5, 4)),
+            dma((1,)), dma((5, 4)),
         ],
         compiler_params=pltpu.CompilerParams(
             collective_id=0, has_side_effects=True, vmem_limit_bytes=56 * 2**20

time: 80.9 us -> 80.2 us (level)
  no operation moved by 1% of the time
where the time goes in v4:
time: 80.2 us; the launch traced here: 79.7 us
  Pallas kernels  78 us (97%)
  local copies, waits for them, and re-layouts  1.67 us (2%)
    pallas_call x1, Pallas kernels, local(): pl.pallas_call(body, out_shape=jax.ShapeDtypeStruct((1024, 128), BF), in_...  78 us
    unnamed x1, local copies, waits for them, and re-layouts  1.67 us

profile of v4, /device:TPU:1, one launch (start us, length us, event | category | flops | bytes accessed | tf_op | source)
XLA Modules:
  0.0 79.7 jit_solution(3148525484680996651)
XLA Ops:
  0.0 78.0 %shard_map.46 = bf16[1024,128]{1,0:T(8,128)(2,1)} custom-call(s32[32,32]{1,0:T(8,128)} %hp.1, s32[32,32]{1,0:T(8,128)} %zp.1, bf16[1024,128]{1,0:T(8,128)(2,1)} %h_hbm.1, bf16[1024,512]{1,0:T(8,128)(2,1)} %z_hbm.1), custom_call_target="tpu_custom_call" | custom-call | flops 4294967296 | bytes 1572864 | tf_op jit(solution)/shard_map/pallas_call | solution.py:431
  78.0 1.7 %copy.6 = bf16[1024,128]{1,0:T(8,128)(2,1)} copy(bf16[1024,128]{1,0:T(8,128)(2,1)} %shard_map.46) | data formatting | bytes 524288

commit v5 on v4

--- a/solution.py
+++ b/solution.py
@@ -14,9 +14,12 @@
 SRC = ((0, 1, 3, 5), (0, 2, 4, 6))
 DST = ((1, 3, 5, 7), (2, 4, 6, 7))
 
-TASKS = ((0, 128, 0, 2), (128, 256, 0, 2), (0, 384, 2, 1), (384, 256, 0, 3), (0, 640, 3, 1), (640, 256, 0, 4), (896, 128, 0, 4))
-
-RING = (1, 2, 3, 4)
+TASKS = (
+    (0, 128, 0, 4), (128, 256, 0, 4), (0, 384, 4, 2), (0, 384, 6, 1),
+    (384, 256, 0, 7), (0, 640, 7, 1), (640, 256, 0, 8), (896, 128, 0, 8),
+)
+
+RING = (4, 5)
 
 
 def body(hp, zp, h_hbm, z_hbm, o_hbm, h_ref, z_ref, o_ref, ht, z1, z2, y, pbuf, xbuf, rss, rsr, cpart, csend, crecv,
@@ -83,7 +86,7 @@
 
     def z1_copy(k, d):
         rows = pl.ds(d * 512, 512)
-        return rcopy(z1.at[k, rows], z1.at[2 + k, rows], z1s.at[0], z1r.at[k, d], ydev[d])
+        return rcopy(z1.at[k, rows], z1.at[4 + k, rows], z1s.at[0], z1r.at[k, d], ydev[d])
 
     loads[1].wait()
     for k in range(2):
@@ -91,10 +94,12 @@
             p = zp[row * 4 + i, col * 2 + k]
             keep = jnp.where(p > 0, 1.0, 0.0).astype(F32)
             blk = z_ref[i * BS:(i + 1) * BS, k * BS:(k + 1) * BS].astype(F32) * keep
-            z1[k, i * BS:(i + 1) * BS, :] = blk.astype(BF)
-        for d in range(2):
-            go(z1_copy(k, d))
-    z2[0] = z1[layer // 2, :, pl.ds(pl.multiple_of(lax.rem(layer, 2) * 128, 128), 128)]
+            for m in range(2):
+                z1[2 * k + m, i * BS:(i + 1) * BS, :] = blk[:, m * 128:(m + 1) * 128].astype(BF)
+        for m in range(2):
+            for d in range(2):
+                go(z1_copy(2 * k + m, d))
+    z2[0] = z1[layer]
 
     def z2_copy(d, s, j):
         start, size = j * 256, 256
@@ -138,8 +143,12 @@
 
     def s1(t):
         h, nh, r0, n, mine, theirs = geometry(t)
-        for k in range(nh):
-            pbuf[h + k, r0:r0 + n] = jnp.dot(ht[r0:r0 + n, :], z1[h + k], preferred_element_type=F32)
+        for k in range(0, nh, 2):
+            w = min(2, nh - k)
+            right = z1[h + k] if w == 1 else jnp.concatenate([z1[h + k], z1[h + k + 1]], axis=1)
+            part = jnp.dot(ht[r0:r0 + n, :], right, preferred_element_type=F32)
+            for m in range(w):
+                pbuf[h + k + m, r0:r0 + n] = part[:, m * 128:(m + 1) * 128]
         go(k_copy(t, theirs))
 
     def k_copy(t, start):
@@ -195,12 +204,12 @@
         rows = half_rows(t, q, (i % 3 == 1) == (i < 3))
         d = 0 if i < 3 else 2
         return rcopy(
-            rss.at[pl.ds(h, nh), rows], rsr.at[d, pl.ds(h, nh), rows], rs_s.at[0], rs_r.at[7 + t if i % 3 == 0 else t], xdev[d]
+            rss.at[pl.ds(h, nh), rows], rsr.at[d, pl.ds(h, nh), rows], rs_s.at[0], rs_r.at[8 + t if i % 3 == 0 else t], xdev[d]
         )
 
     def s6(t):
         h, nh = TASKS[t][2:]
-        await_all(rsr.at[0, pl.ds(h, nh), pl.ds(*quarter(t, x))], rs_r.at[7 + t])
+        await_all(rsr.at[0, pl.ds(h, nh), pl.ds(*quarter(t, x))], rs_r.at[8 + t])
         for i in (0, 3):
             q = x + sign(i)
             rows = half_rows(t, q, i == 3)
@@ -214,11 +223,11 @@
         start, size = quarter(t, lax.rem(q + 4, 4))
         rows = pl.ds(start, size) if i < 2 else half_rows(t, q, i == 3)
         part = y.at[pl.ds(h, nh), rows]
-        return rcopy(part, part, ag_s.at[0], ag_r.at[7 + t if i < 2 else t], xdev[i % 2 * 2])
+        return rcopy(part, part, ag_s.at[0], ag_r.at[8 + t if i < 2 else t], xdev[i % 2 * 2])
 
     def s7(t):
         h, nh, r0, n, mine, theirs = geometry(t)
-        await_all(y.at[pl.ds(h, nh), pl.ds(mine, n // 4)], ag_r.at[7 + t])
+        await_all(y.at[pl.ds(h, nh), pl.ds(mine, n // 4)], ag_r.at[8 + t])
         go(ring_ag(t, 2, x - 1))
         go(ring_ag(t, 3, x + 1))
 
@@ -264,6 +273,7 @@
     s3(0)
     s1(1)
     z1_arrive(0)
+    z1_arrive(1)
     s1(2)
     h_arrive(1, 0)
     s2(1)
@@ -271,53 +281,54 @@
     s2(2)
     h_arrive(1, 2)
     s4(0)
+    z1_arrive(2)
+    s1(3)
     h_arrive(1, 3)
-    s1(3)
-    s6(1)
-    z1_arrive(1)
     s1(4)
+    z1_arrive(3)
+    s1(5)
     h_arrive(2, 0)
-    s6(2)
+    s2(4)
     s2(3)
     h_arrive(2, 1)
-    s2(4)
+    s2(5)
     h_arrive(2, 2)
     z2_start((0, 1, 2, 3,))
     s3(1)
     s3(2)
     h_arrive(2, 3)
-    s1(5)
-    s6(3)
+    s1(6)
+    s6(4)
     h_last(0)
-    s2(5)
-    s6(4)
+    s2(6)
+    s6(5)
     h_last(1)
-    s1(6)
-    s7(1)
-    s7(2)
+    s1(7)
     z2_arrive(0, (0,))
     s3(3)
-    s2(6)
+    s3(4)
+    s2(7)
     z2_arrive(0, (1,))
-    s3(4)
+    s3(5)
     z2_arrive(0, (2,))
-    s3(5)
+    s3(6)
     z2_arrive(0, (3,))
     s4(1)
     s4(2)
     z2_arrive(1, (0,))
-    s7(3)
     s7(4)
-    s3(6)
+    s7(5)
+    s3(7)
     z2_arrive(1, (1,))
     z2_arrive(1, (2,))
     z2_arrive(1, (3,))
-    s4(5)
+    s4(6)
     z2_arrive(2, (0,))
     z2_arrive(2, (1,))
     s4(3)
     s4(4)
-    s4(6)
+    s4(5)
+    s4(7)
     z2_arrive(2, (2,))
     z2_arrive(2, (3,))
     z2_arrive(3, (0,))
@@ -329,6 +340,7 @@
     s5(4)
     s5(5)
     s5(6)
+    s5(7)
 
     def block_of(d):
         t = lax.rem(y_pos + d + 8, 8)
@@ -338,7 +350,8 @@
         rows = pl.ds(j * 256, 256)
         left = jnp.concatenate([z2[s, rows] for s in range(8)], axis=1)
         for q in range(4):
-            part = jnp.dot(left, y[q], preferred_element_type=F32)
+            right = jnp.concatenate([y[2 * q], y[2 * q + 1]], axis=1)
+            part = jnp.dot(left, right, preferred_element_type=F32)
             for b in range(2):
                 cpart[q * 2 + b, rows] = part[:, b * 128:(b + 1) * 128]
 
@@ -415,7 +428,7 @@
     for cp in stores:
         cp.wait()
     await_all(ht.at[pl.ds(0, 896)], hs.at[0])
-    await_all(z1.at[pl.ds(0, 2)], z1s.at[0])
+    await_all(z1.at[pl.ds(0, 4)], z1s.at[0])
     await_all(z2.at[pl.ds(0, 7)], z2s.at[0])
     await_all(pbuf.at[:, pl.ds(0, 512)], ks.at[0])
     await_all(rss.at[:, pl.ds(0, 384)], rs_s.at[0])
@@ -438,24 +451,24 @@
             pltpu.VMEM((1024, 512), BF),
             pltpu.VMEM((1024, 128), BF),
             pltpu.VMEM((1024, 1024), BF),
-            pltpu.VMEM((4, 1024, 256), BF),
             pltpu.VMEM((8, 1024, 128), BF),
-            pltpu.VMEM((4, 1024, 256), BF),
-            pltpu.VMEM((4, 1024, 256), F32),
-            pltpu.VMEM((4, 1024, 256), F32),
-            pltpu.VMEM((4, 1024, 256), BF),
-            pltpu.VMEM((3, 4, 1024, 256), BF),
+            pltpu.VMEM((8, 1024, 128), BF),
+            pltpu.VMEM((8, 1024, 128), BF),
+            pltpu.VMEM((8, 1024, 128), F32),
+            pltpu.VMEM((8, 1024, 128), F32),
+            pltpu.VMEM((8, 1024, 128), BF),
+            pltpu.VMEM((3, 8, 1024, 128), BF),
             pltpu.VMEM((8, 1024, 128), F32),
             pltpu.VMEM((2, 4, 1024, 128), BF),
             pltpu.VMEM((2, 4, 1024, 128), BF),
             dma((2,)), dma((4,)),
             dma((1,)), dma((4, 4)),
-            dma((1,)), dma((2, 2)),
+            dma((1,)), dma((4, 2)),
             dma((1,)), dma((4, 4)),
-            dma((1,)), dma((7,)),
-            dma((1,)), dma((12,)),
-            dma((1,)), dma((12,)),
-            dma((1,)), dma((7,)),
+            dma((1,)), dma((8,)),
+            dma((1,)), dma((14,)),
+            dma((1,)), dma((14,)),
+            dma((1,)), dma((8,)),
             dma((1,)), dma((5, 4)),
         ],
         compiler_params=pltpu.CompilerParams(

time: 80.2 us -> 79.8 us (level)
  the two profiles are of different devices: /device:TPU:1 before, /device:TPU:24 now
where the time goes in v5:
time: 79.8 us; the launch traced here: 79.5 us
  Pallas kernels  77.8 us (97%)
  local copies, waits for them, and re-layouts  1.67 us (2%)
    pallas_call x1, Pallas kernels, local(): pl.pallas_call(body, out_shape=jax.ShapeDtypeStruct((1024, 128), BF), in_...  77.8 us
    unnamed x1, local copies, waits for them, and re-layouts  1.67 us

profile of v5, /device:TPU:24, one launch (start us, length us, event | category | flops | bytes accessed | tf_op | source)
XLA Modules:
  0.0 79.5 jit_solution(5886087913617931150)
XLA Ops:
  0.0 77.8 %shard_map.46 = bf16[1024,128]{1,0:T(8,128)(2,1)} custom-call(s32[32,32]{1,0:T(8,128)} %hp.1, s32[32,32]{1,0:T(8,128)} %zp.1, bf16[1024,128]{1,0:T(8,128)(2,1)} %h_hbm.1, bf16[1024,512]{1,0:T(8,128)(2,1)} %z_hbm.1), custom_call_target="tpu_custom_call" | custom-call | flops 4294967296 | bytes 1572864 | tf_op jit(solution)/shard_map/pallas_call | solution.py:444
  77.8 1.7 %copy.6 = bf16[1024,128]{1,0:T(8,128)(2,1)} copy(bf16[1024,128]{1,0:T(8,128)(2,1)} %shard_map.46) | data formatting | bytes 524288

commit v6 on v5

--- a/solution.py
+++ b/solution.py
@@ -291,9 +291,9 @@
     s2(4)
     s2(3)
     h_arrive(2, 1)
+    z2_start((0, 1, 2, 3,))
     s2(5)
     h_arrive(2, 2)
-    z2_start((0, 1, 2, 3,))
     s3(1)
     s3(2)
     h_arrive(2, 3)

time: 79.8 us -> 79.8 us (level)
  no operation moved by 1% of the time
where the time goes in v6:
time: 79.8 us; the launch traced here: 79.5 us
  Pallas kernels  77.8 us (97%)
  local copies, waits for them, and re-layouts  1.67 us (2%)
    pallas_call x1, Pallas kernels, local(): pl.pallas_call(body, out_shape=jax.ShapeDtypeStruct((1024, 128), BF), in_...  77.8 us
    unnamed x1, local copies, waits for them, and re-layouts  1.67 us

profile of v6, /device:TPU:24, one launch (start us, length us, event | category | flops | bytes accessed | tf_op | source)
XLA Modules:
  0.0 79.5 jit_solution(13505312564141051788)
XLA Ops:
  0.0 77.8 %shard_map.46 = bf16[1024,128]{1,0:T(8,128)(2,1)} custom-call(s32[32,32]{1,0:T(8,128)} %hp.1, s32[32,32]{1,0:T(8,128)} %zp.1, bf16[1024,128]{1,0:T(8,128)(2,1)} %h_hbm.1, bf16[1024,512]{1,0:T(8,128)(2,1)} %z_hbm.1), custom_call_target="tpu_custom_call" | custom-call | flops 4294967296 | bytes 1572864 | tf_op jit(solution)/shard_map/pallas_call | solution.py:444
  77.8 1.7 %copy.6 = bf16[1024,128]{1,0:T(8,128)(2,1)} copy(bf16[1024,128]{1,0:T(8,128)(2,1)} %shard_map.46) | data formatting | bytes 524288
